TPU v7x, 32 devices: a whole 2x2x4 slice. The times are simulated.
32 devices in a mesh: tm: 16 (over z, y, x), rows: 2 (over core).
Axes of the slice: x: 2, y: 2, z: 4, core: 2. Of those that a mesh axis runs over, the one named last changes fastest.
Arguments:
- snapshots: bfloat16 [128, 32, 2048], P('tm', 'rows'), may hold values from -8 to 8
- tile_masks: int32 [128, 4, 16], P('tm', 'rows'), may hold values from 0 to 1, as said below
- widths: int32 [128, 2], P('tm'), may hold values from 1 to 4
Outputs:
- excess_map: float32 [2, 32, 2048], P(None, 'rows', 'tm')
- peak_map: float32 [2, 32, 2048], P(None, 'rows')
Inputs may be any that keep to these rules, and one draw needn't show every extreme that they name: `tile_masks`: 1 keeps the 8 x 128 tile of a snapshot, 0 rejects it.
All inputs are finite; a program needn't handle non-finite values.
Results may differ from a plain program's by a relative error of at most 0.0036.
Values may be sent and summed in bfloat16 or wider, within the bound.
A program may use at most 64 MiB of HBM per device.

v0:
```python
import jax
import jax.numpy as jnp
from jax import lax
from jax.sharding import PartitionSpec as P

HISTORY_FRAMES = 64
RADIUS = 8
TILE_R = 8
TILE_C = 128
threshold = 0.5


def padded(value, sides, width):
    for axis, dim in sides:
        count, length = (lax.axis_size(axis), value.shape[dim])
        up = [(i, (i + 1) % count) for i in range(count - 1)]
        down = [(j, i) for i, j in up]
        last = lax.slice_in_dim(value, length - width, length, axis=dim)
        first = lax.slice_in_dim(value, 0, width, axis=dim)
        before = lax.ppermute(last, axis, up)
        after = lax.ppermute(first, axis, down)
        value = jnp.concatenate([before, value, after], axis=dim)
    return value


def filter_taps(widths):
    sigma_val = widths.astype(jnp.float32)[..., None]
    offsets = jnp.arange(-RADIUS, RADIUS + 1).astype(jnp.float32)
    weights = jnp.exp(-(offsets * offsets) / (2.0 * sigma_val * sigma_val))
    return (weights / jnp.sqrt(jnp.sum(weights * weights, axis=-1, keepdims=True))).astype(
        jnp.bfloat16
    )


def history_band(local_times, back_step):
    target = jnp.arange(local_times)[:, None]
    source = jnp.arange(local_times)[None, :]
    distance = back_step * local_times + target - source
    return ((distance >= 1) & (distance <= HISTORY_FRAMES)).astype(jnp.bfloat16)


def tap_onehot(target_count):
    taps_count = 2 * RADIUS + 1
    source = jnp.arange(target_count + 2 * RADIUS)[:, None, None]
    target = jnp.arange(target_count)[None, :, None]
    return (source - target == jnp.arange(taps_count)[None, None, :]).astype(jnp.float32)


def column_residual(snapshots, tile_masks, widths):
    moved = lax.all_to_all(snapshots, "tm", split_axis=2, concat_axis=0, tiled=True)
    all_masks, all_widths = (
        lax.all_gather(tile_masks, "tm", axis=0, tiled=True),
        lax.all_gather(widths, "tm", axis=0, tiled=True),
    )
    total_times, local_rows, own_cols = moved.shape
    patch_rows = all_masks.shape[1]
    first_col = lax.axis_index("tm") * own_cols
    tile_of = (first_col + jnp.arange(own_cols)) // TILE_C
    pick = (jnp.arange(all_masks.shape[2])[:, None] == tile_of[None, :]).astype(jnp.float32)
    keep_tiles = jnp.einsum("trk,kc->trc", all_masks.astype(jnp.float32), pick)
    keep_pixels = jnp.broadcast_to(
        keep_tiles[:, :, None, :], (total_times, patch_rows, TILE_R, own_cols)
    ).reshape(total_times, local_rows, own_cols)
    pixels = local_rows * own_cols
    keep_flat = keep_pixels.astype(jnp.bfloat16).reshape(total_times, pixels)
    masked = moved.reshape(total_times, pixels) * keep_flat
    block_count = total_times // HISTORY_FRAMES
    own_band = history_band(HISTORY_FRAMES, 0)
    back_band = history_band(HISTORY_FRAMES, 1)
    empty_block = jnp.zeros((1, HISTORY_FRAMES, pixels), jnp.bfloat16)
    value_blocks = masked.reshape(block_count, HISTORY_FRAMES, pixels)
    keep_blocks = keep_flat.reshape(block_count, HISTORY_FRAMES, pixels)
    value_prior = jnp.concatenate([empty_block, value_blocks[:-1]], axis=0)
    keep_prior = jnp.concatenate([empty_block, keep_blocks[:-1]], axis=0)
    window = jnp.einsum("js,bsp->bjp", own_band, value_blocks, preferred_element_type=jnp.float32)
    window = window + jnp.einsum(
        "js,bsp->bjp", back_band, value_prior, preferred_element_type=jnp.float32
    )
    counts = jnp.einsum("js,bsp->bjp", own_band, keep_blocks, preferred_element_type=jnp.float32)
    counts = counts + jnp.einsum(
        "js,bsp->bjp", back_band, keep_prior, preferred_element_type=jnp.float32
    )
    mean_img = (window / jnp.maximum(counts, 1.0)).reshape(total_times, local_rows, own_cols)
    residual = (keep_pixels * (moved.astype(jnp.float32) - mean_img)).astype(jnp.bfloat16)
    return (residual, filter_taps(all_widths).astype(jnp.float32))


def body(snapshots, tile_masks, widths):
    residual, kernel = column_residual(snapshots, tile_masks, widths)
    local_times, local_rows, column_count = residual.shape
    padded_rows = padded(residual, (("rows", 1),), RADIUS)
    row_onehot = tap_onehot(local_rows)
    row_results = []
    for filter_index in range(widths.shape[1]):
        row_weights = jnp.einsum(
            "jik,tk->tij", row_onehot, kernel[:, filter_index], precision=lax.Precision.HIGHEST
        ).astype(jnp.bfloat16)
        row_results.append(
            jnp.einsum(
                "tij,tjc->tic", row_weights, padded_rows, preferred_element_type=jnp.float32
            ).astype(jnp.bfloat16)
        )
    stacked_rows = jnp.stack(row_results)
    padded_cols = padded(stacked_rows, (("tm", 3),), RADIUS)
    column_onehot = tap_onehot(column_count)
    excess_terms = []
    peak_terms = []
    for filter_index in range(widths.shape[1]):
        column_weights = jnp.einsum(
            "jck,tk->tjc", column_onehot, kernel[:, filter_index], precision=lax.Precision.HIGHEST
        ).astype(jnp.bfloat16)
        filtered = jnp.einsum(
            "trj,tjc->trc",
            padded_cols[filter_index],
            column_weights,
            preferred_element_type=jnp.float32,
        )
        excess_terms.append(jnp.sum(jnp.maximum(filtered - threshold, 0.0), axis=0))
        peak_terms.append(jnp.max(filtered, axis=0))
    excess_map = jnp.stack(excess_terms) / local_times
    peak_map = lax.all_gather(jnp.stack(peak_terms), "tm", axis=2, tiled=True)
    return (excess_map, peak_map)


def solution(mesh):
    return jax.shard_map(
        body,
        mesh=mesh,
        in_specs=(P("tm", "rows", None), P("tm", "rows", None), P("tm", None)),
        out_specs=(P(None, "rows", "tm"), P(None, "rows", None)),
        check_vma=False,
    )
```

profile of v0, /device:TPU:0, one launch (start us, length us, event | category | flops | bytes accessed | tf_op | source)
XLA Modules:
  0.0 190.9 jit_solution(9750065384838639887)
XLA Ops:
  0.6 5.3 %copy.35 = bf16[8,16,2048]{1,0,2:T(8,128)(2,1)} copy(bf16[8,16,2048]{2,1,0:T(8,128)(2,1)} %param.3) | data formatting | bytes 1048576 | tf_op args[0]
  6.0 6.4 %reshape.110 = bf16[16,2,8192]{2,1,0:T(2,128)(2,1)} reshape(bf16[2048,8,16]{2,1,0:T(8,128)(2,1)} %bitcast.84) | data formatting | bytes 1048576
  12.4 8.4 %all-to-all-start = ((bf16[16,2,8192]{2,1,0:T(2,128)(2,1)}), bf16[16,2,8192]{2,1,0:T(2,128)(2,1)S(1)}, u32[]{:S(2)}, u32[]{:S(2)}) async-start(bf16[16,2,8192]{2,1,0:T(2,128)(2,1)} %reshape.110), calls=%async_computation | async-start | bytes 1048576 | tf_op jit(solution)/shard_map/all_to_all | solution.py:50
  20.9 43.1 %all_gather.10 = s32[128,2,16]{2,1,0:T(2,128)S(1)} all-gather(s32[8,2,16]{2,1,0:T(2,128)S(1)} %copy-done.4), channel_id=1, replica_groups=mesh['tm'=16,'rows'=2] {'tm'}, dimensions={0}, use_global_device_ids=true | all-gather | bytes 17408 | tf_op jit(solution)/shard_map/all_gather | solution.py:52
  63.9 0.1 copy.33
  64.0 0.2 fusion.59
  64.3 0.1 copy.34
  64.4 0.1 broadcast_bitcast_fusion
  64.5 37.4 %all-gather = s32[16,8,2]{1,2,0:T(2,128)S(1)} all-gather(s32[1,8,2]{1,2,0:T(2,128)S(1)} %bitcast.96), channel_id=1, replica_groups=mesh['tm'=16,'rows'=2] {'tm'}, dimensions={0}, use_global_device_ids=true | all-gather | bytes 1088 | tf_op jit(solution)/shard_map/all_gather | solution.py:53
  101.8 0.1 copy.31
  101.9 0.1 copy.32
  102.0 0.1 reshape.104
  102.1 0.1 multiply_reduce_fusion
  102.2 0.1 divide_convert_fusion
  102.3 0.1 copy.38
  102.4 0.1 broadcast_in_dim.5
  102.5 0.2 convert_element_type.75
  102.8 0.1 copy.58
  102.9 0.1 slice.42
  103.1 0.2 convolution_convert_fusion.5
  103.3 1.2 copy.39
  104.5 0.2 convolution_convert_fusion.4
  104.8 1.2 copy.40
  106.0 1.3 fusion.27
  107.2 0.0 all-to-all-done
  107.2 4.1 %reshape.111 = bf16[2048,8,16]{2,1,0:T(8,128)(2,1)} reshape(bf16[16,2,8192]{2,1,0:T(2,128)(2,1)S(1)} %all-to-all-done) | data formatting | bytes 1048576
  111.4 4.4 %copy.36 = bf16[8,16,16,128]{3,0,1,2:T(8,128)(2,1)S(1)} copy(bf16[8,16,16,128]{1,0,3,2:T(8,128)(2,1)} %bitcast.83) | data formatting | bytes 1048576 | tf_op jit(solution)/shard_map/all_to_all | solution.py:50
  115.8 0.1 bitcast_convert_fusion
  115.9 0.0 copy-start.1
  115.9 0.3 fusion.12
  116.2 0.4 convolution_add_fusion.1
  116.6 0.6 copy-done.1
  117.1 0.4 fusion.5
  117.5 0.2 copy.48
  117.7 0.2 copy.37
  117.9 0.3 fusion.9
  118.2 1.3 collective-permute-start
  119.5 0.0 copy-start.2
  119.6 1.4 collective-permute-start.1
  121.0 3.5 %convolution_convert_fusion.1 = bf16[128,144,128]{2,0,1:T(8,128)(2,1)} fusion(s32[144,128]{1,0:T(8,128)S(1)} %iota_subtract_fusion, bf16[128,2,17]{0,2,1:T(8,128)(2,1)S(1)} %divide_convert_fusion), kind=kOutput, calls=%fused_computation.5 | convolution fusion | flops 82888704 | bytes 4798464 | tf_op jit(solution)/shard_map/jck,tk->tjc/dot_general | solution.py:109
  124.5 0.0 collective-permute-done
  124.5 0.0 collective-permute-done.1
  124.5 0.4 fusion.6
  125.0 0.6 copy-done.3
  125.6 0.4 fusion.7
  126.0 0.0 copy-start
  126.0 0.5 slice_maximum_fusion
  126.5 0.8 copy.41
  127.3 2.1 %collective-permute-start.2 = (bf16[2,128,16,8]{1,3,2,0:T(8,128)(2,1)S(1)}, bf16[2,128,16,8]{1,3,2,0:T(8,128)(2,1)S(1)}, u32[]{:S(2)}, u32[]{:S(2)}) collective-permute-start(bf16[2,128,16,8]{1,3,2,0:T(8,128)(2,1)S(1)} %copy.41), channel_id=1, source_target_pairs={{0,2},{2,4},{4,6},{6,8},{8,10},{10,12},{12,14},{14,16},{16,18},{18... | collective-permute-start | bytes 196616 | tf_op jit(solution)/shard_map/ppermute | solution.py:20
  129.4 0.8 copy.42
  130.2 1.5 collective-permute-start.3
  131.7 3.6 %convolution_convert_fusion = bf16[128,144,128]{2,0,1:T(8,128)(2,1)} fusion(s32[144,128]{1,0:T(8,128)S(1)} %iota_subtract_fusion, bf16[128,2,17]{0,2,1:T(8,128)(2,1)S(1)} %divide_convert_fusion), kind=kOutput, calls=%fused_computation.4 | convolution fusion | flops 82888704 | bytes 4798464 | tf_op jit(solution)/shard_map/jck,tk->tjc/dot_general | solution.py:109
  135.2 0.0 collective-permute-done.2
  135.2 0.8 copy.43
  136.0 0.9 collective-permute-done.3
  136.9 0.8 copy.44
  137.7 0.0 slice-start.1
  137.7 2.4 %pad_maximum_fusion = bf16[2,128,16,144]{3,2,1,0:T(8,128)(2,1)S(1)} fusion(bf16[2,128,16,8]{3,2,1,0:T(8,128)(2,1)S(1)} %copy.44, bf16[1,128,16,128]{3,2,1,0:T(8,128)(2,1)} %copy-done, bf16[1,128,16,128]{3,2,1,0:T(8,128)(2,1)S(1)} %fusion.6, bf16[2,128,16,8]{3,2,1,0:T(8,128)(2,1)S(1)} %copy.43), kind=kLoop, calls=%fused_computation.10 | loop fusion | flops 4718592 | bytes 2359296 | tf_op jit(solution)/shard_map/concatenate | solution.py:22
  140.1 6.6 %fusion.56 = (f32[16,128]{1,0:T(8,128)S(1)}, f32[16,128]{1,0:T(8,128)S(1)}) fusion(bf16[128,144,128]{2,0,1:T(8,128)(2,1)} %convolution_convert_fusion.1, bf16[2,128,16,144]{3,2,1,0:T(8,128)(2,1)S(1)} %pad_maximum_fusion), kind=kOutput, calls=%fused_computation.94 | convolution fusion | flops 76541952 | bytes 5783552 | tf_op jit(solution)/shard_map/trj,tjc->trc/dot_general | solution.py:112
  146.7 0.0 slice-done.1
  146.7 4.3 %fusion.57 = (f32[16,128]{1,0:T(8,128)S(1)}, f32[16,128]{1,0:T(8,128)S(1)}) fusion(bf16[128,144,128]{2,0,1:T(8,128)(2,1)S(1)} %bitcast.88, bf16[2,128,16,144]{3,2,1,0:T(8,128)(2,1)S(1)} %pad_maximum_fusion), kind=kOutput, calls=%fused_computation.95 | convolution fusion | flops 76541952 | bytes 5783552 | tf_op jit(solution)/shard_map/trj,tjc->trc/dot_general | solution.py:112
  151.0 38.6 %all_gather.11 = f32[2,16,2048]{2,1,0:T(8,128)S(1)} all-gather(f32[2,16,128]{2,1,0:T(8,128)S(1)} %pad_maximum_fusion.5), channel_id=1, replica_groups=mesh['tm'=16,'rows'=2] {'tm'}, dimensions={2}, use_global_device_ids=true | all-gather | bytes 278528 | tf_op jit(solution)/shard_map/all_gather | solution.py:121
  189.6 0.6 maximum_multiply_fusion
  190.2 0.7 copy.60
  (21 shorter events, 0.1 us)
Async XLA Ops:
  6.0 14.9 %copy-start.4 = (s32[8,2,16]{2,1,0:T(2,128)S(1)}, s32[8,2,16]{2,1,0:T(2,128)}, u32[]{:S(2)}) copy-start(s32[8,2,16]{2,1,0:T(2,128)} %param.4) | copy-start | bytes 3076
  12.4 52.1 %copy-start.5 = (s32[8,2]{0,1:T(2,128)S(1)}, s32[8,2]{0,1:T(2,128)}, u32[]{:S(2)}) copy-start(s32[8,2]{0,1:T(2,128)} %param.5) | copy-start | bytes 196
  12.4 94.8 %all-to-all-start = ((bf16[16,2,8192]{2,1,0:T(2,128)(2,1)}), bf16[16,2,8192]{2,1,0:T(2,128)(2,1)S(1)}, u32[]{:S(2)}, u32[]{:S(2)}) async-start(bf16[16,2,8192]{2,1,0:T(2,128)(2,1)} %reshape.110), calls=%async_computation | async-start | bytes 1048576 | tf_op jit(solution)/shard_map/all_to_all | solution.py:50
  115.9 1.2 copy-start.1
  118.2 6.3 %collective-permute-start = (bf16[128,8,128]{2,1,0:T(8,128)(2,1)S(1)}, bf16[128,8,128]{2,1,0:T(8,128)(2,1)S(1)}, u32[]{:S(2)}, u32[]{:S(2)}) collective-permute-start(bf16[128,8,128]{2,1,0:T(8,128)(2,1)S(1)} %get-tuple-element.8), channel_id=1, source_target_pairs={{0,1},{2,3},{4,5},{6,7},{8,9},{10,11},{12,13},{14,15},{16,17},{18,... | collective-permute-start | bytes 786440 | tf_op jit(solution)/shard_map/ppermute | solution.py:20
  119.5 5.0 %copy-start.2 = (bf16[128,32,16]{1,2,0:T(8,128)(2,1)S(1)}, bf16[128,32,16]{1,2,0:T(8,128)(2,1)}, u32[]{:S(2)}) copy-start(bf16[128,32,16]{1,2,0:T(8,128)(2,1)} %copy.39) | copy-start | bytes 393220
  119.6 5.0 %collective-permute-start.1 = (bf16[128,8,128]{2,1,0:T(8,128)(2,1)S(1)}, bf16[128,8,128]{2,1,0:T(8,128)(2,1)S(1)}, u32[]{:S(2)}, u32[]{:S(2)}) collective-permute-start(bf16[128,8,128]{2,1,0:T(8,128)(2,1)S(1)} %get-tuple-element.9), channel_id=1, source_target_pairs={{1,0},{3,2},{5,4},{7,6},{9,8},{11,10},{13,12},{15,14},{17,16},{19,... | collective-permute-start | bytes 786440 | tf_op jit(solution)/shard_map/ppermute | solution.py:21
  124.5 1.0 copy-start.3
  126.0 10.0 %copy-start = (bf16[1,128,16,128]{3,2,1,0:T(8,128)(2,1)}, bf16[1,128,16,128]{3,2,1,0:T(8,128)(2,1)S(1)}, u32[]{:S(2)}) copy-start(bf16[1,128,16,128]{3,2,1,0:T(8,128)(2,1)S(1)} %fusion.7) | copy-start | bytes 1572868
  127.3 8.0 %collective-permute-start.2 = (bf16[2,128,16,8]{1,3,2,0:T(8,128)(2,1)S(1)}, bf16[2,128,16,8]{1,3,2,0:T(8,128)(2,1)S(1)}, u32[]{:S(2)}, u32[]{:S(2)}) collective-permute-start(bf16[2,128,16,8]{1,3,2,0:T(8,128)(2,1)S(1)} %copy.41), channel_id=1, source_target_pairs={{0,2},{2,4},{4,6},{6,8},{8,10},{10,12},{12,14},{14,16},{16,18},{18... | collective-permute-start | bytes 196616 | tf_op jit(solution)/shard_map/ppermute | solution.py:20
  130.2 6.7 %collective-permute-start.3 = (bf16[2,128,16,8]{1,3,2,0:T(8,128)(2,1)S(1)}, bf16[2,128,16,8]{1,3,2,0:T(8,128)(2,1)S(1)}, u32[]{:S(2)}, u32[]{:S(2)}) collective-permute-start(bf16[2,128,16,8]{1,3,2,0:T(8,128)(2,1)S(1)} %copy.42), channel_id=1, source_target_pairs={{2,0},{4,2},{6,4},{8,6},{10,8},{12,10},{14,12},{16,14},{18,16},{20... | collective-permute-start | bytes 196616 | tf_op jit(solution)/shard_map/ppermute | solution.py:21
  135.2 11.4 %slice-start = ((s8[4718592]{0:T(1024)(128)(4,1)}), s8[524288]{0:T(1024)(128)(4,1)S(1)}, s32[]{:S(2)}) async-start(s8[4718592]{0:T(1024)(128)(4,1)} %bitcast.87), calls=%async_computation.1 | async-start | bytes 1048576
  137.7 9.0 %slice-start.1 = ((s8[4718592]{0:T(1024)(128)(4,1)}), s8[4194304]{0:T(1024)(128)(4,1)S(1)}, s32[]{:S(2)}) async-start(s8[4718592]{0:T(1024)(128)(4,1)} %bitcast.87), calls=%async_computation.2 | async-start | bytes 8388608
where the time goes:
time: 192 us; the launch traced here: 191 us
  blocking collectives  119 us (62%)
  local copies, waits for them, and re-layouts  29.4 us (15%)
  matrix products  21.9 us (11%)
  starting transfers between devices  14.7 us (8%)
  other arithmetic  4.06 us (2%)
    all_gather x1, blocking collectives, column_residual(): lax.all_gather(tile_masks, 'tm', axis=0, tiled=True)  43.1 us
    all_gather x1, blocking collectives, body(): peak_map = lax.all_gather(jnp.stack(peak_terms), 'tm', axis=2, tiled=True)  38.6 us
    all_gather x1, blocking collectives, column_residual(): lax.all_gather(widths, 'tm', axis=0, tiled=True)  37.4 us
    unnamed x22, local copies, waits for them, and re-layouts  18.1 us
    dot_general x2, matrix products, body(): jnp.einsum('trj,tjc->trc', padded_cols[filter_index], column_weights, pre...  10.9 us
    all_to_all x1, starting transfers between devices, column_residual(): lax.all_to_all(snapshots, 'tm', split_axis=2, concat_axis=0, tiled=True)  8.44 us
    dot_general x2, matrix products, body(): jnp.einsum('jck,tk->tjc', column_onehot, kernel[:, filter_index], precisi...  7.14 us
    all_to_all x1, local copies, waits for them, and re-layouts, column_residual(): lax.all_to_all(snapshots, 'tm', split_axis=2, concat_axis=0, tiled=True)  4.41 us
  transfers between devices with their start and end apart: 5, of which 1 were waited for; matrix products, arithmetic and copies ran while one was open for 8% of the time, Pallas kernels for 0%

commit v1 on v0

--- a/solution.py
+++ b/solution.py
@@ -8,6 +8,28 @@
 TILE_R = 8
 TILE_C = 128
 threshold = 0.5
+
+
+def laid_out(blocks, dim):
+    shape = list(blocks.shape[1:])
+    shape[dim] *= blocks.shape[0]
+    return jnp.moveaxis(blocks, 0, dim).reshape(shape)
+
+
+def ring_gather(x, axis, dim):
+    peers = lax.axis_size(axis)
+    pairs = [(i, (i + 1) % peers) for i in range(peers)]
+    back = [(b, a) for a, b in pairs]
+    lower, upper = ([], [])
+    for step in range(peers - 1):
+        if step % 2 == 0:
+            lower.append(lax.ppermute(lower[-1] if lower else x, axis, pairs))
+        else:
+            upper.append(lax.ppermute(upper[-1] if upper else x, axis, back))
+    tiles = jnp.stack([*lower[::-1], x, *upper])
+    shift = lax.axis_index(axis) - len(lower)
+    tiles = tiles[(jnp.arange(peers) - shift) % peers]
+    return laid_out(tiles, dim)
 
 
 def padded(value, sides, width):
@@ -50,7 +72,7 @@
     moved = lax.all_to_all(snapshots, "tm", split_axis=2, concat_axis=0, tiled=True)
     all_masks, all_widths = (
         lax.all_gather(tile_masks, "tm", axis=0, tiled=True),
-        lax.all_gather(widths, "tm", axis=0, tiled=True),
+        ring_gather(widths, "tm", 0),
     )
     total_times, local_rows, own_cols = moved.shape
     patch_rows = all_masks.shape[1]

time: 192 us -> 212 us (1.10)
  starting transfers between devices: 14.7 us -> 51.8 us
  blocking collectives: 119 us -> 87.6 us
  waiting for transfers between devices: 0.88 us -> 15.4 us
    ppermute x0 -> x15, starting transfers between devices: none -> 42.7 us  [the longest x7 37.8 us: ring_gather(): upper.append(lax.ppermute(upper[-1] if upper else x, axis, back))]
    all_gather x1 -> x0, blocking collectives: 37.4 us -> none  [column_residual(): lax.all_gather(widths, 'tm', axis=0, tiled=True)]
    ppermute x0 -> x15, waiting for transfers between devices: none -> 14.4 us  [the longest x8 14.4 us: ring_gather(): lower.append(lax.ppermute(lower[-1] if lower else x, axis, pairs))]
    all_gather x1, blocking collectives: 38.6 us -> 44.6 us  [body(): peak_map = lax.all_gather(jnp.stack(peak_terms), 'tm', axis=2, tiled=True)]
    all_to_all x1, starting transfers between devices: 8.44 us -> 3.57 us  [column_residual(): lax.all_to_all(snapshots, 'tm', split_axis=2, concat_axis=0, tiled=True)]
    unnamed x22 -> x35, local copies, waits for them, and re-layouts: 18.1 us -> 18.4 us
  transfers between devices with their start and end apart: 5 -> 20, of which waited for: 1 -> 8; matrix products, arithmetic and copies ran while one was open for 8% -> 12% of each run, Pallas kernels for 0% -> 0%
where the time goes in v1:
time: 212 us; the launch traced here: 211 us
  blocking collectives  87.6 us (41%)
  starting transfers between devices  51.8 us (24%)
  local copies, waits for them, and re-layouts  30.3 us (14%)
  matrix products  20.9 us (10%)
  waiting for transfers between devices  15.4 us (7%)
  other arithmetic  4.08 us (2%)
    all_gather x1, blocking collectives, body(): peak_map = lax.all_gather(jnp.stack(peak_terms), 'tm', axis=2, tiled=True)  44.6 us
    all_gather x1, blocking collectives, column_residual(): lax.all_gather(tile_masks, 'tm', axis=0, tiled=True)  42.9 us
    ppermute x7, starting transfers between devices, ring_gather(): upper.append(lax.ppermute(upper[-1] if upper else x, axis, back))  37.8 us
    unnamed x35, local copies, waits for them, and re-layouts  18.4 us
    ppermute x8, waiting for transfers between devices, ring_gather(): lower.append(lax.ppermute(lower[-1] if lower else x, axis, pairs))  14.4 us
    dot_general x2, matrix products, body(): jnp.einsum('trj,tjc->trc', padded_cols[filter_index], column_weights, pre...  10.9 us
    dot_general x2, matrix products, body(): jnp.einsum('jck,tk->tjc', column_onehot, kernel[:, filter_index], precisi...  7.17 us
    ppermute x8, starting transfers between devices, ring_gather(): lower.append(lax.ppermute(lower[-1] if lower else x, axis, pairs))  4.92 us
  transfers between devices with their start and end apart: 20, of which 8 were waited for; matrix products, arithmetic and copies ran while one was open for 12% of the time, Pallas kernels for 0%

profile of v1, /device:TPU:0, one launch (start us, length us, event | category | flops | bytes accessed | tf_op | source)
XLA Modules:
  0.0 211.2 jit_solution(10607718019085281664)
XLA Ops:
  0.6 3.0 %collective-permute-start = (s32[8,2]{0,1:T(2,128)}, s32[8,2]{0,1:T(2,128)S(1)}, u32[]{:S(2)}, u32[]{:S(2)}) collective-permute-start(s32[8,2]{0,1:T(2,128)} %param.5), channel_id=1, source_target_pairs={{0,2},{2,4},{4,6},{6,8},{8,10},{10,12},{12,14},{14,16},{16,18},{18... | collective-permute-start | bytes 200 | tf_op jit(solution)/shard_map/ppermute | solution.py:26
  3.6 4.1 %collective-permute-start.8 = (s32[8,2]{0,1:T(2,128)}, s32[8,2]{0,1:T(2,128)S(1)}, u32[]{:S(2)}, u32[]{:S(2)}) collective-permute-start(s32[8,2]{0,1:T(2,128)} %param.5), channel_id=1, source_target_pairs={{2,0},{4,2},{6,4},{8,6},{10,8},{12,10},{14,12},{16,14},{18,16},{20... | collective-permute-start | bytes 200 | tf_op jit(solution)/shard_map/ppermute | solution.py:28
  7.7 5.3 %copy.50 = bf16[8,16,2048]{1,0,2:T(8,128)(2,1)} copy(bf16[8,16,2048]{2,1,0:T(8,128)(2,1)} %param.3) | data formatting | bytes 1048576 | tf_op args[0]
  13.0 6.5 %reshape.172 = bf16[16,2,8192]{2,1,0:T(2,128)(2,1)} reshape(bf16[2048,8,16]{2,1,0:T(8,128)(2,1)} %bitcast.117) | data formatting | bytes 1048576
  19.5 3.6 %all-to-all-start = ((bf16[16,2,8192]{2,1,0:T(2,128)(2,1)}), bf16[16,2,8192]{2,1,0:T(2,128)(2,1)S(1)}, u32[]{:S(2)}, u32[]{:S(2)}) async-start(bf16[16,2,8192]{2,1,0:T(2,128)(2,1)} %reshape.172), calls=%async_computation | async-start | bytes 1048576 | tf_op jit(solution)/shard_map/all_to_all | solution.py:72
  23.2 42.9 %all_gather.6 = s32[128,2,16]{2,1,0:T(2,128)S(1)} all-gather(s32[8,2,16]{2,1,0:T(2,128)S(1)} %copy-done.3), channel_id=1, replica_groups=mesh['tm'=16,'rows'=2] {'tm'}, dimensions={0}, use_global_device_ids=true | all-gather | bytes 17408 | tf_op jit(solution)/shard_map/all_gather | solution.py:74
  66.2 0.2 fusion.61
  66.4 0.1 copy.53
  66.6 0.2 convert_element_type.83
  66.9 0.1 copy.73
  67.0 0.3 fusion.27
  67.3 0.1 copy.49
  67.6 1.9 collective-permute-start.1
  69.5 0.1 slice.42
  69.6 5.2 %collective-permute-done.1 = s32[8,2]{0,1:T(2,128)S(1)} collective-permute-done((s32[8,2]{0,1:T(2,128)S(1)}, s32[8,2]{0,1:T(2,128)S(1)}, u32[]{:S(2)}, u32[]{:S(2)}) %collective-permute-start.1) | collective-permute-done | bytes 96 | tf_op jit(solution)/shard_map/ppermute | solution.py:26
  74.8 5.6 %collective-permute-start.9 = (s32[8,2]{0,1:T(2,128)S(1)}, s32[8,2]{0,1:T(2,128)S(1)}, u32[]{:S(2)}, u32[]{:S(2)}) collective-permute-start(s32[8,2]{0,1:T(2,128)S(1)} %collective-permute-done.8), channel_id=1, source_target_pairs={{2,0},{4,2},{6,4},{8,6},{10,8},{12,10},{14,12},{16,14},{18,16},{20... | collective-permute-start | bytes 200 | tf_op jit(solution)/shard_map/ppermute | solution.py:28
  80.4 1.5 collective-permute-done.2
  82.0 5.6 %collective-permute-start.10 = (s32[8,2]{0,1:T(2,128)S(1)}, s32[8,2]{0,1:T(2,128)S(1)}, u32[]{:S(2)}, u32[]{:S(2)}) collective-permute-start(s32[8,2]{0,1:T(2,128)S(1)} %collective-permute-done.9), channel_id=1, source_target_pairs={{2,0},{4,2},{6,4},{8,6},{10,8},{12,10},{14,12},{16,14},{18,16},{20... | collective-permute-start | bytes 200 | tf_op jit(solution)/shard_map/ppermute | solution.py:28
  87.6 1.5 collective-permute-done.3
  89.1 5.6 %collective-permute-start.11 = (s32[8,2]{0,1:T(2,128)S(1)}, s32[8,2]{0,1:T(2,128)S(1)}, u32[]{:S(2)}, u32[]{:S(2)}) collective-permute-start(s32[8,2]{0,1:T(2,128)S(1)} %collective-permute-done.10), channel_id=1, source_target_pairs={{2,0},{4,2},{6,4},{8,6},{10,8},{12,10},{14,12},{16,14},{18,16},{20... | collective-permute-start | bytes 200 | tf_op jit(solution)/shard_map/ppermute | solution.py:28
  94.7 1.5 collective-permute-done.4
  96.3 5.6 %collective-permute-start.12 = (s32[8,2]{0,1:T(2,128)S(1)}, s32[8,2]{0,1:T(2,128)S(1)}, u32[]{:S(2)}, u32[]{:S(2)}) collective-permute-start(s32[8,2]{0,1:T(2,128)S(1)} %collective-permute-done.11), channel_id=1, source_target_pairs={{2,0},{4,2},{6,4},{8,6},{10,8},{12,10},{14,12},{16,14},{18,16},{20... | collective-permute-start | bytes 200 | tf_op jit(solution)/shard_map/ppermute | solution.py:28
  101.9 1.5 collective-permute-done.5
  103.5 5.6 %collective-permute-start.13 = (s32[8,2]{0,1:T(2,128)S(1)}, s32[8,2]{0,1:T(2,128)S(1)}, u32[]{:S(2)}, u32[]{:S(2)}) collective-permute-start(s32[8,2]{0,1:T(2,128)S(1)} %collective-permute-done.12), channel_id=1, source_target_pairs={{2,0},{4,2},{6,4},{8,6},{10,8},{12,10},{14,12},{16,14},{18,16},{20... | collective-permute-start | bytes 200 | tf_op jit(solution)/shard_map/ppermute | solution.py:28
  109.1 1.5 collective-permute-done.6
  110.6 5.6 %collective-permute-start.14 = (s32[8,2]{0,1:T(2,128)S(1)}, s32[8,2]{0,1:T(2,128)S(1)}, u32[]{:S(2)}, u32[]{:S(2)}) collective-permute-start(s32[8,2]{0,1:T(2,128)S(1)} %collective-permute-done.13), channel_id=1, source_target_pairs={{2,0},{4,2},{6,4},{8,6},{10,8},{12,10},{14,12},{16,14},{18,16},{20... | collective-permute-start | bytes 200 | tf_op jit(solution)/shard_map/ppermute | solution.py:28
  116.3 1.5 collective-permute-done.7
  118.0 0.6 gather_fusion
  118.8 0.1 multiply_reduce_fusion
  119.0 0.2 convolution_convert_fusion.5
  119.3 1.2 copy.54
  120.5 0.2 convolution_convert_fusion.4
  120.8 1.2 copy.55
  122.0 4.1 %reshape.173 = bf16[2048,8,16]{2,1,0:T(8,128)(2,1)} reshape(bf16[16,2,8192]{2,1,0:T(2,128)(2,1)S(1)} %all-to-all-done) | data formatting | bytes 1048576
  126.1 4.4 %copy.51 = bf16[8,16,16,128]{3,0,1,2:T(8,128)(2,1)S(1)} copy(bf16[8,16,16,128]{1,0,3,2:T(8,128)(2,1)} %bitcast.116) | data formatting | bytes 1048576 | tf_op jit(solution)/shard_map/all_to_all | solution.py:72
  130.5 0.1 bitcast_convert_fusion
  130.6 0.3 fusion.12
  130.9 0.4 convolution_add_fusion.1
  131.2 0.3 fusion.5
  131.6 0.2 copy.63
  131.8 0.2 copy.52
  132.0 0.3 fusion.9
  132.3 1.3 collective-permute-start.15
  133.6 1.6 collective-permute-start.16
  135.3 3.5 %convolution_convert_fusion.1 = bf16[128,144,128]{2,0,1:T(8,128)(2,1)} fusion(s32[144,128]{1,0:T(8,128)S(1)} %iota_subtract_fusion, bf16[128,2,17]{0,2,1:T(8,128)(2,1)S(1)} %divide_convert_fusion), kind=kOutput, calls=%fused_computation.6 | convolution fusion | flops 82888704 | bytes 4798464 | tf_op jit(solution)/shard_map/jck,tk->tjc/dot_general | solution.py:131
  138.8 0.4 fusion.6
  139.3 0.6 copy-done.2
  139.8 0.4 fusion.7
  140.3 0.8 copy-done
  141.1 0.5 slice_maximum_fusion
  141.6 0.8 copy.56
  142.4 1.3 collective-permute-start.17
  143.7 0.8 copy.57
  144.5 1.3 collective-permute-start.18
  145.8 3.6 %convolution_convert_fusion = bf16[128,144,128]{2,0,1:T(8,128)(2,1)} fusion(s32[144,128]{1,0:T(8,128)S(1)} %iota_subtract_fusion, bf16[128,2,17]{0,2,1:T(8,128)(2,1)S(1)} %divide_convert_fusion), kind=kOutput, calls=%fused_computation.5 | convolution fusion | flops 82888704 | bytes 4798464 | tf_op jit(solution)/shard_map/jck,tk->tjc/dot_general | solution.py:131
  149.4 0.8 copy.58
  150.2 1.0 collective-permute-done.18
  151.2 0.8 copy.59
  151.9 2.4 %pad_maximum_fusion = bf16[2,128,16,144]{3,2,1,0:T(8,128)(2,1)S(1)} fusion(bf16[2,128,16,8]{3,2,1,0:T(8,128)(2,1)S(1)} %copy.59, bf16[1,128,16,128]{3,2,1,0:T(8,128)(2,1)} %copy-done, bf16[1,128,16,128]{3,2,1,0:T(8,128)(2,1)S(1)} %fusion.6, bf16[2,128,16,8]{3,2,1,0:T(8,128)(2,1)S(1)} %copy.58), kind=kLoop, calls=%fused_computation.11 | loop fusion | flops 4718592 | bytes 2359296 | tf_op jit(solution)/shard_map/concatenate | solution.py:44
  154.3 6.6 %fusion.58 = (f32[16,128]{1,0:T(8,128)S(1)}, f32[16,128]{1,0:T(8,128)S(1)}) fusion(bf16[128,144,128]{2,0,1:T(8,128)(2,1)} %convolution_convert_fusion.1, bf16[2,128,16,144]{3,2,1,0:T(8,128)(2,1)S(1)} %pad_maximum_fusion), kind=kOutput, calls=%fused_computation.118 | convolution fusion | flops 76541952 | bytes 5783552 | tf_op jit(solution)/shard_map/trj,tjc->trc/dot_general | solution.py:134
  161.0 4.3 %fusion.59 = (f32[16,128]{1,0:T(8,128)S(1)}, f32[16,128]{1,0:T(8,128)S(1)}) fusion(bf16[128,144,128]{2,0,1:T(8,128)(2,1)S(1)} %bitcast.121, bf16[2,128,16,144]{3,2,1,0:T(8,128)(2,1)S(1)} %pad_maximum_fusion), kind=kOutput, calls=%fused_computation.119 | convolution fusion | flops 76541952 | bytes 5783552 | tf_op jit(solution)/shard_map/trj,tjc->trc/dot_general | solution.py:134
  165.3 44.6 %all_gather.7 = f32[2,16,2048]{2,1,0:T(8,128)S(1)} all-gather(f32[2,16,128]{2,1,0:T(8,128)S(1)} %pad_maximum_fusion.5), channel_id=1, replica_groups=mesh['tm'=16,'rows'=2] {'tm'}, dimensions={2}, use_global_device_ids=true | all-gather | bytes 278528 | tf_op jit(solution)/shard_map/all_gather | solution.py:143
  209.9 0.6 maximum_multiply_fusion
  210.5 0.7 copy.90
  (67 shorter events, 0.9 us)
Async XLA Ops:
  0.6 66.9 %collective-permute-start = (s32[8,2]{0,1:T(2,128)}, s32[8,2]{0,1:T(2,128)S(1)}, u32[]{:S(2)}, u32[]{:S(2)}) collective-permute-start(s32[8,2]{0,1:T(2,128)} %param.5), channel_id=1, source_target_pairs={{0,2},{2,4},{4,6},{6,8},{8,10},{10,12},{12,14},{14,16},{16,18},{18... | collective-permute-start | bytes 200 | tf_op jit(solution)/shard_map/ppermute | solution.py:26
  3.6 71.2 %collective-permute-start.8 = (s32[8,2]{0,1:T(2,128)}, s32[8,2]{0,1:T(2,128)S(1)}, u32[]{:S(2)}, u32[]{:S(2)}) collective-permute-start(s32[8,2]{0,1:T(2,128)} %param.5), channel_id=1, source_target_pairs={{2,0},{4,2},{6,4},{8,6},{10,8},{12,10},{14,12},{16,14},{18,16},{20... | collective-permute-start | bytes 200 | tf_op jit(solution)/shard_map/ppermute | solution.py:28
  13.0 10.1 %copy-start.3 = (s32[8,2,16]{2,1,0:T(2,128)S(1)}, s32[8,2,16]{2,1,0:T(2,128)}, u32[]{:S(2)}) copy-start(s32[8,2,16]{2,1,0:T(2,128)} %param.4) | copy-start | bytes 3076
  19.5 102.5 %all-to-all-start = ((bf16[16,2,8192]{2,1,0:T(2,128)(2,1)}), bf16[16,2,8192]{2,1,0:T(2,128)(2,1)S(1)}, u32[]{:S(2)}, u32[]{:S(2)}) async-start(bf16[16,2,8192]{2,1,0:T(2,128)(2,1)} %reshape.172), calls=%async_computation | async-start | bytes 1048576 | tf_op jit(solution)/shard_map/all_to_all | solution.py:72
  66.9 51.0 %copy-start.4 = (s32[8,2]{0,1:T(2,128)S(1)}, s32[8,2]{0,1:T(2,128)}, u32[]{:S(2)}) copy-start(s32[8,2]{0,1:T(2,128)} %param.5) | copy-start | bytes 196
  67.6 7.2 %collective-permute-start.1 = (s32[8,2]{0,1:T(2,128)S(1)}, s32[8,2]{0,1:T(2,128)S(1)}, u32[]{:S(2)}, u32[]{:S(2)}) collective-permute-start(s32[8,2]{0,1:T(2,128)S(1)} %collective-permute-done), channel_id=1, source_target_pairs={{0,2},{2,4},{4,6},{6,8},{8,10},{10,12},{12,14},{14,16},{16,18},{18... | collective-permute-start | bytes 200 | tf_op jit(solution)/shard_map/ppermute | solution.py:26
  74.8 7.2 %collective-permute-start.2 = (s32[8,2]{0,1:T(2,128)S(1)}, s32[8,2]{0,1:T(2,128)S(1)}, u32[]{:S(2)}, u32[]{:S(2)}) collective-permute-start(s32[8,2]{0,1:T(2,128)S(1)} %collective-permute-done.1), channel_id=1, source_target_pairs={{0,2},{2,4},{4,6},{6,8},{8,10},{10,12},{12,14},{14,16},{16,18},{18... | collective-permute-start | bytes 200 | tf_op jit(solution)/shard_map/ppermute | solution.py:26
  74.8 7.2 %collective-permute-start.9 = (s32[8,2]{0,1:T(2,128)S(1)}, s32[8,2]{0,1:T(2,128)S(1)}, u32[]{:S(2)}, u32[]{:S(2)}) collective-permute-start(s32[8,2]{0,1:T(2,128)S(1)} %collective-permute-done.8), channel_id=1, source_target_pairs={{2,0},{4,2},{6,4},{8,6},{10,8},{12,10},{14,12},{16,14},{18,16},{20... | collective-permute-start | bytes 200 | tf_op jit(solution)/shard_map/ppermute | solution.py:28
  81.9 7.2 %collective-permute-start.3 = (s32[8,2]{0,1:T(2,128)S(1)}, s32[8,2]{0,1:T(2,128)S(1)}, u32[]{:S(2)}, u32[]{:S(2)}) collective-permute-start(s32[8,2]{0,1:T(2,128)S(1)} %collective-permute-done.2), channel_id=1, source_target_pairs={{0,2},{2,4},{4,6},{6,8},{8,10},{10,12},{12,14},{14,16},{16,18},{18... | collective-permute-start | bytes 200 | tf_op jit(solution)/shard_map/ppermute | solution.py:26
  82.0 7.2 %collective-permute-start.10 = (s32[8,2]{0,1:T(2,128)S(1)}, s32[8,2]{0,1:T(2,128)S(1)}, u32[]{:S(2)}, u32[]{:S(2)}) collective-permute-start(s32[8,2]{0,1:T(2,128)S(1)} %collective-permute-done.9), channel_id=1, source_target_pairs={{2,0},{4,2},{6,4},{8,6},{10,8},{12,10},{14,12},{16,14},{18,16},{20... | collective-permute-start | bytes 200 | tf_op jit(solution)/shard_map/ppermute | solution.py:28
  89.1 7.2 %collective-permute-start.4 = (s32[8,2]{0,1:T(2,128)S(1)}, s32[8,2]{0,1:T(2,128)S(1)}, u32[]{:S(2)}, u32[]{:S(2)}) collective-permute-start(s32[8,2]{0,1:T(2,128)S(1)} %collective-permute-done.3), channel_id=1, source_target_pairs={{0,2},{2,4},{4,6},{6,8},{8,10},{10,12},{12,14},{14,16},{16,18},{18... | collective-permute-start | bytes 200 | tf_op jit(solution)/shard_map/ppermute | solution.py:26
  89.1 7.2 %collective-permute-start.11 = (s32[8,2]{0,1:T(2,128)S(1)}, s32[8,2]{0,1:T(2,128)S(1)}, u32[]{:S(2)}, u32[]{:S(2)}) collective-permute-start(s32[8,2]{0,1:T(2,128)S(1)} %collective-permute-done.10), channel_id=1, source_target_pairs={{2,0},{4,2},{6,4},{8,6},{10,8},{12,10},{14,12},{16,14},{18,16},{20... | collective-permute-start | bytes 200 | tf_op jit(solution)/shard_map/ppermute | solution.py:28
  96.3 7.2 %collective-permute-start.5 = (s32[8,2]{0,1:T(2,128)S(1)}, s32[8,2]{0,1:T(2,128)S(1)}, u32[]{:S(2)}, u32[]{:S(2)}) collective-permute-start(s32[8,2]{0,1:T(2,128)S(1)} %collective-permute-done.4), channel_id=1, source_target_pairs={{0,2},{2,4},{4,6},{6,8},{8,10},{10,12},{12,14},{14,16},{16,18},{18... | collective-permute-start | bytes 200 | tf_op jit(solution)/shard_map/ppermute | solution.py:26
  96.3 7.2 %collective-permute-start.12 = (s32[8,2]{0,1:T(2,128)S(1)}, s32[8,2]{0,1:T(2,128)S(1)}, u32[]{:S(2)}, u32[]{:S(2)}) collective-permute-start(s32[8,2]{0,1:T(2,128)S(1)} %collective-permute-done.11), channel_id=1, source_target_pairs={{2,0},{4,2},{6,4},{8,6},{10,8},{12,10},{14,12},{16,14},{18,16},{20... | collective-permute-start | bytes 200 | tf_op jit(solution)/shard_map/ppermute | solution.py:28
  103.5 7.2 %collective-permute-start.6 = (s32[8,2]{0,1:T(2,128)S(1)}, s32[8,2]{0,1:T(2,128)S(1)}, u32[]{:S(2)}, u32[]{:S(2)}) collective-permute-start(s32[8,2]{0,1:T(2,128)S(1)} %collective-permute-done.5), channel_id=1, source_target_pairs={{0,2},{2,4},{4,6},{6,8},{8,10},{10,12},{12,14},{14,16},{16,18},{18... | collective-permute-start | bytes 200 | tf_op jit(solution)/shard_map/ppermute | solution.py:26
  103.5 7.2 %collective-permute-start.13 = (s32[8,2]{0,1:T(2,128)S(1)}, s32[8,2]{0,1:T(2,128)S(1)}, u32[]{:S(2)}, u32[]{:S(2)}) collective-permute-start(s32[8,2]{0,1:T(2,128)S(1)} %collective-permute-done.12), channel_id=1, source_target_pairs={{2,0},{4,2},{6,4},{8,6},{10,8},{12,10},{14,12},{16,14},{18,16},{20... | collective-permute-start | bytes 200 | tf_op jit(solution)/shard_map/ppermute | solution.py:28
  110.6 7.2 %collective-permute-start.7 = (s32[8,2]{0,1:T(2,128)S(1)}, s32[8,2]{0,1:T(2,128)S(1)}, u32[]{:S(2)}, u32[]{:S(2)}) collective-permute-start(s32[8,2]{0,1:T(2,128)S(1)} %collective-permute-done.6), channel_id=1, source_target_pairs={{0,2},{2,4},{4,6},{6,8},{8,10},{10,12},{12,14},{14,16},{16,18},{18... | collective-permute-start | bytes 200 | tf_op jit(solution)/shard_map/ppermute | solution.py:26
  110.6 7.3 %collective-permute-start.14 = (s32[8,2]{0,1:T(2,128)S(1)}, s32[8,2]{0,1:T(2,128)S(1)}, u32[]{:S(2)}, u32[]{:S(2)}) collective-permute-start(s32[8,2]{0,1:T(2,128)S(1)} %collective-permute-done.13), channel_id=1, source_target_pairs={{2,0},{4,2},{6,4},{8,6},{10,8},{12,10},{14,12},{16,14},{18,16},{20... | collective-permute-start | bytes 200 | tf_op jit(solution)/shard_map/ppermute | solution.py:28
  132.3 6.5 %collective-permute-start.15 = (bf16[128,8,128]{2,1,0:T(8,128)(2,1)S(1)}, bf16[128,8,128]{2,1,0:T(8,128)(2,1)S(1)}, u32[]{:S(2)}, u32[]{:S(2)}) collective-permute-start(bf16[128,8,128]{2,1,0:T(8,128)(2,1)S(1)} %get-tuple-element.8), channel_id=1, source_target_pairs={{0,1},{2,3},{4,5},{6,7},{8,9},{10,11},{12,13},{14,15},{16,17},{18,... | collective-permute-start | bytes 786440 | tf_op jit(solution)/shard_map/ppermute | solution.py:42
  133.6 5.2 %copy-start.1 = (bf16[128,32,16]{1,2,0:T(8,128)(2,1)S(1)}, bf16[128,32,16]{1,2,0:T(8,128)(2,1)}, u32[]{:S(2)}) copy-start(bf16[128,32,16]{1,2,0:T(8,128)(2,1)} %copy.54) | copy-start | bytes 393220
  133.6 5.2 %collective-permute-start.16 = (bf16[128,8,128]{2,1,0:T(8,128)(2,1)S(1)}, bf16[128,8,128]{2,1,0:T(8,128)(2,1)S(1)}, u32[]{:S(2)}, u32[]{:S(2)}) collective-permute-start(bf16[128,8,128]{2,1,0:T(8,128)(2,1)S(1)} %get-tuple-element.9), channel_id=1, source_target_pairs={{1,0},{3,2},{5,4},{7,6},{9,8},{11,10},{13,12},{15,14},{17,16},{19,... | collective-permute-start | bytes 786440 | tf_op jit(solution)/shard_map/ppermute | solution.py:43
  138.8 1.0 copy-start.2
  140.3 0.8 copy-start
  142.4 7.0 %collective-permute-start.17 = (bf16[2,128,16,8]{1,3,2,0:T(8,128)(2,1)S(1)}, bf16[2,128,16,8]{1,3,2,0:T(8,128)(2,1)S(1)}, u32[]{:S(2)}, u32[]{:S(2)}) collective-permute-start(bf16[2,128,16,8]{1,3,2,0:T(8,128)(2,1)S(1)} %copy.56), channel_id=1, source_target_pairs={{0,2},{2,4},{4,6},{6,8},{8,10},{10,12},{12,14},{14,16},{16,18},{18... | collective-permute-start | bytes 196616 | tf_op jit(solution)/shard_map/ppermute | solution.py:42
  144.5 6.7 %collective-permute-start.18 = (bf16[2,128,16,8]{1,3,2,0:T(8,128)(2,1)S(1)}, bf16[2,128,16,8]{1,3,2,0:T(8,128)(2,1)S(1)}, u32[]{:S(2)}, u32[]{:S(2)}) collective-permute-start(bf16[2,128,16,8]{1,3,2,0:T(8,128)(2,1)S(1)} %copy.57), channel_id=1, source_target_pairs={{2,0},{4,2},{6,4},{8,6},{10,8},{12,10},{14,12},{16,14},{18,16},{20... | collective-permute-start | bytes 196616 | tf_op jit(solution)/shard_map/ppermute | solution.py:43
  149.4 11.5 %slice-start = ((s8[4718592]{0:T(1024)(128)(4,1)}), s8[524288]{0:T(1024)(128)(4,1)S(1)}, s32[]{:S(2)}) async-start(s8[4718592]{0:T(1024)(128)(4,1)} %bitcast.120), calls=%async_computation.1 | async-start | bytes 1048576
  151.9 9.0 %slice-start.1 = ((s8[4718592]{0:T(1024)(128)(4,1)}), s8[4194304]{0:T(1024)(128)(4,1)S(1)}, s32[]{:S(2)}) async-start(s8[4718592]{0:T(1024)(128)(4,1)} %bitcast.120), calls=%async_computation.2 | async-start | bytes 8388608
